TPU v7x, 32 devices: a whole 2x2x4 slice. The times are simulated.
32 devices in a mesh: groups: 2 (over x), expert: 16 (over z, y, core).
Axes of the slice: x: 2, y: 2, z: 4, core: 2. Of those that a mesh axis runs over, the one named last changes fastest.
Arguments:
- block_input: bfloat16 [2048, 1152], P(('groups', 'expert')), parts along dimension 0, may hold values from -6 to 6
- probe_bits: int32 [2048, 1152], P(('groups', 'expert')), parts along dimension 0, may hold values from 0 to 1
- query_rows: bfloat16 [2048, 1152], P(('groups', 'expert')), parts along dimension 0, may hold values from -8 to 8
- key_rows: bfloat16 [2048, 1152], P(('groups', 'expert')), parts along dimension 0, may hold values from -8 to 8
- value_rows: bfloat16 [2048, 1152], P(('groups', 'expert')), parts along dimension 0, may hold values from -6 to 6
- query_tangent: bfloat16 [2048, 1152], P(('groups', 'expert')), parts along dimension 0, may hold values from -6 to 6
- key_tangent: bfloat16 [2048, 1152], P(('groups', 'expert')), parts along dimension 0, may hold values from -6 to 6
- value_tangent: bfloat16 [2048, 1152], P(('groups', 'expert')), parts along dimension 0, may hold values from -6 to 6
- output_weight: bfloat16 [1152, 1152], replicated, may hold values from -0.1875 to 0.1875
- expert_up: bfloat16 [1152, 73728], P(None, 'expert'), may hold values from -0.1875 to 0.1875
- expert_down: bfloat16 [1152, 73728], P(None, 'expert'), may hold values from -0.09375 to 0.09375
- expert_ids: int32 [2048, 2], P(('groups', 'expert')), parts along dimension 0, may hold values from 0 to 15, all different within a row
- gate_weights: float32 [2048, 2], P(('groups', 'expert')), parts along dimension 0, may hold values from 0.1 to 0.9
Outputs:
- block_output: bfloat16 [2048, 1152], P(('groups', 'expert')), parts along dimension 0
- output_tangent: bfloat16 [2048, 1152], P(('groups', 'expert')), parts along dimension 0
- probe_dot: float32 [2048], P(('groups', 'expert')), parts along dimension 0
There are 2 independent parts, one for each index of `groups`. A program takes and returns all parts, laid end to end along the dimension named above; an argument that names none is the same for every part. Nothing has to cross between parts.
Inputs may be any that keep to these rules, and one draw needn't show every extreme that they name: `expert_ids`: each row names 2 different experts.
All inputs are finite; a program needn't handle non-finite values.
Results may differ from a plain program's by a relative error of at most 0.0053.
Values may be sent and summed in bfloat16 or wider, within the bound.
A program may use at most 128 MiB of HBM per device.

v0:
```python
import jax
import jax.numpy as jnp
from jax import lax
from jax.sharding import PartitionSpec as P

D = 1152
HEADS = 16
EXPERTS = 16
TOP = 2
LENGTH = 512


CUBIC_COEF = 0.044715
TANH_SCALE = 0.7978845608028654
NORM_EPS = 1e-06


def from_partner(block, axis, stride):
    count = lax.axis_size(axis)
    route = []
    for low in range(count):
        high = low | 1 << stride
        if high != low and high < count:
            route += [(low, high), (high, low)]
    return lax.ppermute(block, axis, route)


def gelu_pair(preact):
    inner_arg = TANH_SCALE * (preact + CUBIC_COEF * preact * preact * preact)
    tanh_value = jnp.tanh(inner_arg)
    activation = 0.5 * preact * (1.0 + tanh_value)
    derivative = 0.5 * (1.0 + tanh_value) + 0.5 * preact * (
        1.0 - tanh_value * tanh_value
    ) * TANH_SCALE * (1.0 + 3.0 * CUBIC_COEF * preact * preact)
    return (activation, derivative)


def norm_pair(hidden, tangent):
    average = jnp.mean(hidden, axis=-1, keepdims=True)
    centered = hidden - average
    variance = jnp.mean(centered * centered, axis=-1, keepdims=True)
    inverse = lax.rsqrt(variance + NORM_EPS)
    normed = centered * inverse
    tangent_centered = tangent - jnp.mean(tangent, axis=-1, keepdims=True)
    normed_tangent = inverse * (
        tangent_centered - normed * jnp.mean(normed * tangent_centered, axis=-1, keepdims=True)
    )
    return (normed, normed_tangent)


def attend_heads(query_heads, query_slope, key_heads, value_heads, key_slope, value_slope):
    score_scale = (D // HEADS) ** (-0.5)
    scores = (
        jnp.einsum("thd,shd->hts", query_heads, key_heads, preferred_element_type=jnp.float32)
        * score_scale
    )
    joined_query = jnp.concatenate([query_slope, query_heads], axis=2)
    joined_key = jnp.concatenate([key_heads, key_slope], axis=2)
    score_tangent = (
        jnp.einsum("thd,shd->hts", joined_query, joined_key, preferred_element_type=jnp.float32)
        * score_scale
    )
    row_max = jnp.max(scores, axis=-1, keepdims=True)
    exponent = jnp.exp(scores - row_max)
    weights = exponent / jnp.sum(exponent, axis=-1, keepdims=True)
    weight_tangent = weights * (
        score_tangent - jnp.sum(weights * score_tangent, axis=-1, keepdims=True)
    )
    weights_low = weights.astype(jnp.bfloat16)
    tangent_low = weight_tangent.astype(jnp.bfloat16)
    mixture = jnp.einsum(
        "hts,shd->thd", weights_low, value_heads, preferred_element_type=jnp.float32
    )
    mixture_tangent = jnp.einsum(
        "hts,shd->thd", tangent_low, value_heads, preferred_element_type=jnp.float32
    ) + jnp.einsum("hts,shd->thd", weights_low, value_slope, preferred_element_type=jnp.float32)
    return (mixture.astype(jnp.bfloat16), mixture_tangent.astype(jnp.bfloat16))


def send_back(main_part, slope_part):
    return (
        lax.all_to_all(main_part, "expert", split_axis=0, concat_axis=0, tiled=True),
        lax.all_to_all(slope_part, "expert", split_axis=0, concat_axis=0, tiled=True),
    )


def owner_partials(main_rows, slope_rows, expert_up, expert_down):
    preact = jnp.dot(main_rows, expert_up, preferred_element_type=jnp.float32)
    preact_tangent = jnp.dot(slope_rows, expert_up, preferred_element_type=jnp.float32)
    activation, derivative = gelu_pair(preact)
    act_low = activation.astype(jnp.bfloat16)
    act_slope = (derivative * preact_tangent).astype(jnp.bfloat16)
    contract = (((1,), (1,)), ((), ()))
    produced = lax.dot_general(
        act_low, expert_down, contract, preferred_element_type=jnp.float32
    ).astype(jnp.bfloat16)
    produced_slope = lax.dot_general(
        act_slope, expert_down, contract, preferred_element_type=jnp.float32
    ).astype(jnp.bfloat16)
    return (produced, produced_slope)


def per_device(
    block_input,
    probe_bits,
    query_rows,
    key_rows,
    value_rows,
    query_tangent,
    key_tangent,
    value_tangent,
    output_weight,
    expert_up,
    expert_down,
    expert_ids,
    gate_weights,
):
    row_count = block_input.shape[0]
    head_dim = D // HEADS
    image_steps = (LENGTH // row_count).bit_length() - 1
    key_set = jnp.stack([key_rows, value_rows, key_tangent, value_tangent])
    for bit_index in range(image_steps):
        key_set = jnp.concatenate([key_set, from_partner(key_set, "expert", bit_index)], axis=1)
    key_heads = key_set.reshape(4, -1, HEADS, head_dim)
    mixture, mixture_tangent = attend_heads(
        query_rows.reshape(row_count, HEADS, head_dim),
        query_tangent.reshape(row_count, HEADS, head_dim),
        key_heads[0],
        key_heads[1],
        key_heads[2],
        key_heads[3],
    )
    mixture = mixture.reshape(row_count, D)
    mixture_tangent = mixture_tangent.reshape(row_count, D)
    devices = lax.axis_size("expert")
    owners = devices // EXPERTS
    sign_values = (2 * probe_bits - 1).astype(jnp.float32)
    hidden = block_input.astype(jnp.float32) + jnp.dot(
        mixture, output_weight, preferred_element_type=jnp.float32
    )
    hidden_tangent = sign_values + jnp.dot(
        mixture_tangent, output_weight, preferred_element_type=jnp.float32
    )
    normed, normed_tangent = norm_pair(hidden, hidden_tangent)
    normed_low = normed.astype(jnp.bfloat16)
    normed_slope = normed_tangent.astype(jnp.bfloat16)
    capacity = row_count * TOP // EXPERTS
    flat_ids = expert_ids.reshape(-1)
    one_hot = (flat_ids[:, None] == jnp.arange(EXPERTS, dtype=jnp.int32)[None, :]).astype(jnp.int32)
    order_rank = jnp.sum(one_hot * (jnp.cumsum(one_hot, axis=0) - 1), axis=1)
    retained = order_rank < capacity
    target_slot = jnp.where(retained, flat_ids * capacity + order_rank, EXPERTS * capacity)
    selected = jnp.arange(EXPERTS * capacity, dtype=jnp.int32)[:, None] == target_slot[None, :]
    dispatch_matrix = (
        selected.reshape(EXPERTS * capacity, row_count, TOP)
        .astype(jnp.float32)
        .sum(axis=2)
        .astype(jnp.bfloat16)
    )
    gate_kept = jnp.where(retained, gate_weights.reshape(-1), 0.0)
    mixing = (
        jnp.where(selected, gate_kept[None, :], 0.0)
        .reshape(EXPERTS * capacity, row_count, TOP)
        .sum(axis=2)
    )
    slot_main = jnp.dot(dispatch_matrix, normed_low, preferred_element_type=jnp.float32).astype(
        jnp.bfloat16
    )
    slot_slope = jnp.dot(dispatch_matrix, normed_slope, preferred_element_type=jnp.float32).astype(
        jnp.bfloat16
    )

    def spread(slots):
        return jnp.broadcast_to(
            slots.reshape(EXPERTS, 1, capacity, D), (EXPERTS, owners, capacity, D)
        ).reshape(devices, capacity, D)

    outgoing = (spread(slot_main), spread(slot_slope))
    received = (
        lax.all_to_all(outgoing[0], "expert", split_axis=0, concat_axis=0, tiled=True),
        lax.all_to_all(outgoing[1], "expert", split_axis=0, concat_axis=0, tiled=True),
    )
    shape_now = received[0].shape
    produced, produced_slope = owner_partials(
        received[0].reshape(-1, D), received[1].reshape(-1, D), expert_up, expert_down
    )
    returned_main, returned_slope = send_back(
        produced.reshape(shape_now), produced_slope.reshape(shape_now)
    )

    def fold_owners(returned):
        return (
            returned.reshape(EXPERTS, owners, capacity, D)
            .astype(jnp.float32)
            .sum(axis=1)
            .reshape(EXPERTS * capacity, D)
        )

    contract = (((0,), (0,)), ((), ()))
    expert_mix = lax.dot_general(
        mixing,
        fold_owners(returned_main),
        contract,
        precision=lax.Precision.HIGHEST,
        preferred_element_type=jnp.float32,
    )
    expert_mix_tangent = lax.dot_general(
        mixing,
        fold_owners(returned_slope),
        contract,
        precision=lax.Precision.HIGHEST,
        preferred_element_type=jnp.float32,
    )
    block_output = (hidden + expert_mix).astype(jnp.bfloat16)
    full_tangent = hidden_tangent + expert_mix_tangent
    probe_dot = jnp.sum(sign_values * full_tangent, axis=1) * D ** (-0.5)
    return (block_output, full_tangent.astype(jnp.bfloat16), probe_dot)


def solution(mesh):
    return jax.shard_map(
        per_device,
        mesh=mesh,
        in_specs=(
            P(("groups", "expert"), None),
            P(("groups", "expert"), None),
            P(("groups", "expert"), None),
            P(("groups", "expert"), None),
            P(("groups", "expert"), None),
            P(("groups", "expert"), None),
            P(("groups", "expert"), None),
            P(("groups", "expert"), None),
            P(),
            P(None, "expert"),
            P(None, "expert"),
            P(("groups", "expert"), None),
            P(("groups", "expert"), None),
        ),
        out_specs=(
            P(("groups", "expert"), None),
            P(("groups", "expert"), None),
            P(("groups", "expert")),
        ),
        check_vma=False,
    )
```

profile of v0, /device:TPU:0, one launch (start us, length us, event | category | flops | bytes accessed | tf_op | source)
XLA Modules:
  0.0 202.0 jit_solution(2198194273065550136)
XLA Ops:
  5.5 3.0 %collective-permute-start.1 = (bf16[4,128,1152]{2,1,0:T(8,128)(2,1)S(1)}, bf16[4,128,1152]{2,1,0:T(8,128)(2,1)S(1)}, u32[]{:S(2)}, u32[]{:S(2)}) collective-permute-start(bf16[4,128,1152]{2,1,0:T(8,128)(2,1)S(1)} %pad_maximum_fusion.2), channel_id=1, source_target_pairs={{0,2},{2,0},{1,3},{3,1},{4,6},{6,4},{5,7},{7,5},{8,10},{10,8},{9,1... | collective-permute-start | bytes 3538952 | tf_op jit(solution)/shard_map/ppermute | solution.py:25
  8.4 26.3 %collective-permute-done.1 = bf16[4,128,1152]{2,1,0:T(8,128)(2,1)S(1)} collective-permute-done((bf16[4,128,1152]{2,1,0:T(8,128)(2,1)S(1)}, bf16[4,128,1152]{2,1,0:T(8,128)(2,1)S(1)}, u32[]{:S(2)}, u32[]{:S(2)}) %collective-permute-start.1) | collective-permute-done | bytes 1179680 | tf_op jit(solution)/shard_map/ppermute | solution.py:25
  60.0 29.6 %collective-permute-done.2 = bf16[4,256,1152]{2,1,0:T(8,128)(2,1)} collective-permute-done((bf16[4,256,1152]{2,1,0:T(8,128)(2,1)}, bf16[4,256,1152]{2,1,0:T(8,128)(2,1)}, u32[]{:S(2)}, u32[]{:S(2)}) %collective-permute-start.2) | collective-permute-done | bytes 2359328 | tf_op jit(solution)/shard_map/ppermute | solution.py:25
  89.6 2.9 %pad_maximum_fusion = bf16[4,512,1152]{2,1,0:T(8,128)(2,1)S(1)} fusion(bf16[4,256,1152]{2,1,0:T(8,128)(2,1)} %collective-permute-done.2, bf16[4,128,1152]{2,1,0:T(8,128)(2,1)} %copy-done.1, bf16[4,64,1152]{2,1,0:T(8,128)(2,1)S(1)} %collective-permute-done, bf16[1,64,1152]{2,1,0:T(8,128)(2,1)S(1)} %bitcast.66, bf16[1,64,1152]{2,1,0:T(8,128)(2,1)S(1)} %bitcast.70, ...), kind=kLoop, calls=%fused_computation.3 | loop fusion | flops 33030144 | bytes 9437184 | tf_op jit(solution)/shard_map/concatenate | solution.py:123
  92.5 2.3 %fusion.72 = (bf16[1,512,1152]{2,1,0:T(8,128)(2,1)}, bf16[1,512,1152]{2,1,0:T(8,128)(2,1)}, bf16[1,512,1152]{2,1,0:T(8,128)(2,1)}, bf16[1,512,1152]{2,1,0:T(8,128)(2,1)}) fusion(bf16[4,512,1152]{2,1,0:T(8,128)(2,1)S(1)} %pad_maximum_fusion), kind=kLoop, calls=%fused_computation.108 | loop fusion | bytes 9437184 | tf_op jit(solution)/shard_map/slice | solution.py:130
  94.8 2.4 %copy.37 = bf16[1,512,1152]{1,2,0:T(8,128)(2,1)} copy(bf16[1,512,1152]{2,1,0:T(8,128)(2,1)} %get-tuple-element.8) | data formatting | bytes 2359296 | tf_op jit(solution)/shard_map/slice | solution.py:129
  97.2 2.4 %copy.38 = bf16[1,512,1152]{1,2,0:T(8,128)(2,1)} copy(bf16[1,512,1152]{2,1,0:T(8,128)(2,1)} %get-tuple-element.7) | data formatting | bytes 2359296 | tf_op jit(solution)/shard_map/slice | solution.py:128
  99.7 3.3 %fusion.73 = (f32[16,64]{1,0:T(8,128)S(1)}, f32[16,64,512]{2,1,0:T(8,128)}) fusion(bf16[512,16,72]{0,2,1:T(8,128)(2,1)} %bitcast.81, bf16[64,16,72]{2,1,0:T(8,128)(2,1)S(1)} %copy-done.9), kind=kOutput, calls=%fused_computation.109 | convolution fusion | flops 77070848 | bytes 3428352 | tf_op jit(solution)/shard_map/sub | solution.py:64
  103.0 2.5 %fusion.27 = bf16[64,16,72]{2,0,1:T(8,128)(2,1)S(1)} fusion(bf16[512,16,72]{0,2,1:T(8,128)(2,1)} %bitcast.79, f32[16,64,512]{2,1,0:T(8,128)} %get-tuple-element.12, f32[16,64]{1,0:T(8,128)S(1)} %get-tuple-element.11), kind=kOutput, calls=%fused_computation.46 | convolution fusion | flops 76619776 | bytes 3428352 | tf_op jit(solution)/shard_map/hts,shd->thd/dot_general | solution.py:71
  107.2 2.5 %copy.50 = bf16[1,512,1152]{1,2,0:T(8,128)(2,1)} copy(bf16[1,512,1152]{2,1,0:T(8,128)(2,1)} %get-tuple-element.6) | data formatting | bytes 2359296 | tf_op jit(solution)/shard_map/slice | solution.py:131
  109.6 3.3 %fusion.34 = f32[16,72,64]{1,2,0:T(8,128)} fusion(bf16[512,16,72]{0,2,1:T(8,128)(2,1)} %bitcast.84, f32[16,64,512]{2,1,0:T(8,128)} %get-tuple-element.12, f32[16,64]{1,0:T(8,128)S(1)} %get-tuple-element.11), kind=kOutput, calls=%fused_computation.55 | convolution fusion | flops 76546048 | bytes 3575808 | tf_op jit(solution)/shard_map/hts,shd->thd/dot_general | solution.py:76
  112.9 2.5 %copy.49 = bf16[1,512,1152]{1,2,0:T(8,128)(2,1)} copy(bf16[1,512,1152]{2,1,0:T(8,128)(2,1)} %get-tuple-element.5) | data formatting | bytes 2359296 | tf_op jit(solution)/shard_map/slice | solution.py:130
  115.4 3.3 %multiply_reduce_fusion = (f32[16,64]{1,0:T(8,128)S(1)}, f32[16,64,512]{2,1,0:T(8,128)S(1)}) fusion(f32[16,64,512]{2,1,0:T(8,128)} %get-tuple-element.12, f32[16,64]{1,0:T(8,128)S(1)} %get-tuple-element.11, bf16[512,16,72]{0,2,1:T(8,128)(2,1)} %bitcast.83, bf16[512,16,72]{0,2,1:T(8,128)(2,1)} %bitcast.82, bf16[64,16,72]{2,0,1:T(8,128)(2,1)S(1)} %copy-done.10, ...), kind=kOutput, calls=%fused_computation.35 | convolution fusion | flops 158399488 | bytes 6856704 | tf_op jit(solution)/shard_map/thd,shd->hts/dot_general | solution.py:60
  125.3 5.8 %all-to-all-start = ((bf16[16,8,1152]{2,1,0:T(8,128)(2,1)}), bf16[16,8,1152]{2,1,0:T(8,128)(2,1)S(1)}, u32[]{:S(2)}, u32[]{:S(2)}) async-start(bf16[16,8,1152]{2,1,0:T(8,128)(2,1)} %fusion.11), calls=%async_computation | async-start | bytes 589824 | tf_op jit(solution)/shard_map/all_to_all | solution.py:180
  133.8 7.9 %all-to-all-done = bf16[16,8,1152]{2,1,0:T(8,128)(2,1)S(1)} async-done(((bf16[16,8,1152]{2,1,0:T(8,128)(2,1)}), bf16[16,8,1152]{2,1,0:T(8,128)(2,1)S(1)}, u32[]{:S(2)}, u32[]{:S(2)}) %all-to-all-start) | async-done | bytes 294944 | tf_op jit(solution)/shard_map/all_to_all | solution.py:180
  141.7 4.4 %all-to-all-start.2 = ((bf16[16,8,1152]{2,1,0:T(8,128)(2,1)}), bf16[16,8,1152]{2,1,0:T(8,128)(2,1)}, u32[]{:S(2)}, u32[]{:S(2)}) async-start(bf16[16,8,1152]{2,1,0:T(8,128)(2,1)} %fusion.12), calls=%async_computation.2 | async-start | bytes 589824 | tf_op jit(solution)/shard_map/all_to_all | solution.py:181
  146.1 7.1 %fusion.41 = f32[128,4608]{1,0:T(8,128)} fusion(bf16[1152,4608]{1,0:T(8,128)(2,1)} %param.22, bf16[16,8,1152]{2,1,0:T(8,128)(2,1)S(1)} %all-to-all-done), kind=kOutput, calls=%fused_computation.61 | convolution fusion | flops 1358954496 | bytes 13271040 | tf_op jit(solution)/shard_map/dot_general | solution.py:88
  153.2 3.3 %all-to-all-done.2 = bf16[16,8,1152]{2,1,0:T(8,128)(2,1)} async-done(((bf16[16,8,1152]{2,1,0:T(8,128)(2,1)}), bf16[16,8,1152]{2,1,0:T(8,128)(2,1)}, u32[]{:S(2)}, u32[]{:S(2)}) %all-to-all-start.2) | async-done | bytes 294944 | tf_op jit(solution)/shard_map/all_to_all | solution.py:181
  156.5 14.4 %fusion.14 = bf16[16,8,1152]{2,1,0:T(8,128)(2,1)} fusion(bf16[1152,4608]{1,0:T(8,128)(2,1)} %param.23, bf16[1152,4608]{1,0:T(8,128)(2,1)} %param.22, f32[128,4608]{1,0:T(8,128)} %fusion.41, bf16[16,8,1152]{2,1,0:T(8,128)(2,1)} %all-to-all-done.2), kind=kOutput, calls=%fused_computation.28 | convolution fusion | flops 2729263104 | bytes 24182784 | tf_op jit(solution)/shard_map/dot_general | solution.py:97
  170.8 3.5 %all-to-all-start.3 = ((bf16[16,8,1152]{2,1,0:T(8,128)(2,1)}), bf16[16,8,1152]{2,1,0:T(8,128)(2,1)S(1)}, u32[]{:S(2)}, u32[]{:S(2)}) async-start(bf16[16,8,1152]{2,1,0:T(8,128)(2,1)} %fusion.14), calls=%async_computation.3 | async-start | bytes 589824 | tf_op jit(solution)/shard_map/all_to_all | solution.py:83
  174.4 8.6 %fusion.13 = bf16[16,8,1152]{2,1,0:T(8,128)(2,1)} fusion(bf16[1152,4608]{1,0:T(8,128)(2,1)} %param.23, f32[128,4608]{1,0:T(8,128)} %fusion.41), kind=kOutput, calls=%fused_computation.27 | convolution fusion | flops 1364410368 | bytes 13271040 | tf_op jit(solution)/shard_map/dot_general | solution.py:94
  185.6 4.1 %all-to-all-start.1 = ((bf16[16,8,1152]{2,1,0:T(8,128)(2,1)}), bf16[16,8,1152]{2,1,0:T(8,128)(2,1)S(1)}, u32[]{:S(2)}, u32[]{:S(2)}) async-start(bf16[16,8,1152]{2,1,0:T(8,128)(2,1)} %fusion.13), calls=%async_computation.1 | async-start | bytes 589824 | tf_op jit(solution)/shard_map/all_to_all | solution.py:82
  189.7 2.1 %multiply_reduce_fusion.1 = (f32[64]{0:T(128)S(1)}, bf16[64,1152]{1,0:T(8,128)(2,1)}) fusion(s32[64,1152]{1,0:T(8,128)} %param.14, f32[64,1152]{1,0:T(8,128)S(1)} %get-tuple-element.18, f32[128,64]{0,1:T(8,128)} %get-tuple-element.4, bf16[16,8,1152]{2,1,0:T(8,128)(2,1)} %copy-done.7), kind=kOutput, calls=%fused_computation.63 | convolution fusion | flops 113762240 | bytes 1065216 | tf_op jit(solution)/shard_map/dot_general | solution.py:207
  192.4 7.9 %all-to-all-done.1 = bf16[16,8,1152]{2,1,0:T(8,128)(2,1)S(1)} async-done(((bf16[16,8,1152]{2,1,0:T(8,128)(2,1)}), bf16[16,8,1152]{2,1,0:T(8,128)(2,1)S(1)}, u32[]{:S(2)}, u32[]{:S(2)}) %all-to-all-start.1) | async-done | bytes 294944 | tf_op jit(solution)/shard_map/all_to_all | solution.py:82
  (81 shorter events, 45.7 us)
Async XLA Ops:
  0.6 105.3 %copy-start = (bf16[1152,1152]{1,0:T(8,128)(2,1)S(1)}, bf16[1152,1152]{1,0:T(8,128)(2,1)}, u32[]{:S(2)}) copy-start(bf16[1152,1152]{1,0:T(8,128)(2,1)} %param.21) | copy-start | bytes 7962628
  0.6 34.0 %copy-start.2 = (bf16[64,1152]{1,0:T(8,128)(2,1)S(1)}, bf16[64,1152]{1,0:T(8,128)(2,1)}, u32[]{:S(2)}) copy-start(bf16[64,1152]{1,0:T(8,128)(2,1)} %param.20) | copy-start | bytes 442372
  0.7 34.0 %copy-start.3 = (bf16[64,1152]{1,0:T(8,128)(2,1)S(1)}, bf16[64,1152]{1,0:T(8,128)(2,1)}, u32[]{:S(2)}) copy-start(bf16[64,1152]{1,0:T(8,128)(2,1)} %param.19) | copy-start | bytes 442372
  0.7 34.0 %copy-start.4 = (bf16[64,1152]{1,0:T(8,128)(2,1)S(1)}, bf16[64,1152]{1,0:T(8,128)(2,1)}, u32[]{:S(2)}) copy-start(bf16[64,1152]{1,0:T(8,128)(2,1)} %param.17) | copy-start | bytes 442372
  0.7 34.0 %copy-start.5 = (bf16[64,1152]{1,0:T(8,128)(2,1)S(1)}, bf16[64,1152]{1,0:T(8,128)(2,1)}, u32[]{:S(2)}) copy-start(bf16[64,1152]{1,0:T(8,128)(2,1)} %param.16) | copy-start | bytes 442372
  2.1 2.1 %collective-permute-start = (bf16[4,64,1152]{2,1,0:T(8,128)(2,1)S(1)}, bf16[4,64,1152]{2,1,0:T(8,128)(2,1)S(1)}, u32[]{:S(2)}, u32[]{:S(2)}) collective-permute-start(bf16[4,64,1152]{2,1,0:T(8,128)(2,1)S(1)} %pad_maximum_fusion.3), channel_id=1, source_target_pairs={{0,1},{1,0},{2,3},{3,2},{4,5},{5,4},{6,7},{7,6},{8,9},{9,8},{10,11... | collective-permute-start | bytes 1769480 | tf_op jit(solution)/shard_map/ppermute | solution.py:25
  5.4 34.9 %copy-start.15 = (s32[64,2]{0,1:T(2,128)S(1)}, s32[64,2]{0,1:T(2,128)}, u32[]{:S(2)}) copy-start(s32[64,2]{0,1:T(2,128)} %param.24) | copy-start | bytes 1540
  5.4 44.1 %copy-start.16 = (f32[64,2]{0,1:T(2,128)S(1)}, f32[64,2]{0,1:T(2,128)}, u32[]{:S(2)}) copy-start(f32[64,2]{0,1:T(2,128)} %param.25) | copy-start | bytes 1540
  5.5 29.2 %collective-permute-start.1 = (bf16[4,128,1152]{2,1,0:T(8,128)(2,1)S(1)}, bf16[4,128,1152]{2,1,0:T(8,128)(2,1)S(1)}, u32[]{:S(2)}, u32[]{:S(2)}) collective-permute-start(bf16[4,128,1152]{2,1,0:T(8,128)(2,1)S(1)} %pad_maximum_fusion.2), channel_id=1, source_target_pairs={{0,2},{2,0},{1,3},{3,1},{4,6},{6,4},{5,7},{7,5},{8,10},{10,8},{9,1... | collective-permute-start | bytes 3538952 | tf_op jit(solution)/shard_map/ppermute | solution.py:25
  36.5 53.1 %collective-permute-start.2 = (bf16[4,256,1152]{2,1,0:T(8,128)(2,1)}, bf16[4,256,1152]{2,1,0:T(8,128)(2,1)}, u32[]{:S(2)}, u32[]{:S(2)}) collective-permute-start(bf16[4,256,1152]{2,1,0:T(8,128)(2,1)} %pad_maximum_fusion.1), channel_id=1, source_target_pairs={{0,4},{4,0},{1,5},{5,1},{2,6},{6,2},{3,7},{7,3},{8,12},{12,8},{9,1... | collective-permute-start | bytes 7077896 | tf_op jit(solution)/shard_map/ppermute | solution.py:25
  94.8 4.9 %copy-start.9 = (bf16[64,16,72]{2,1,0:T(8,128)(2,1)S(1)}, bf16[64,16,72]{2,1,0:T(8,128)(2,1)}, u32[]{:S(2)}) copy-start(bf16[64,16,72]{2,1,0:T(8,128)(2,1)} %reshape.119) | copy-start | bytes 442372
  102.9 12.5 %copy-start.18 = (f32[16,64]{1,0:T(8,128)}, f32[16,64]{1,0:T(8,128)S(1)}, u32[]{:S(2)}) copy-start(f32[16,64]{1,0:T(8,128)S(1)} %get-tuple-element.11) | copy-start | bytes 12292
  103.0 3.0 %copy-start.12 = (bf16[64,1152]{1,0:T(8,128)(2,1)S(1)}, bf16[64,1152]{1,0:T(8,128)(2,1)}, u32[]{:S(2)}) copy-start(bf16[64,1152]{1,0:T(8,128)(2,1)} %param.13) | copy-start | bytes 442372
  112.9 2.5 %copy-start.10 = (bf16[64,16,72]{2,0,1:T(8,128)(2,1)S(1)}, bf16[64,16,72]{2,0,1:T(8,128)(2,1)}, u32[]{:S(2)}) copy-start(bf16[64,16,72]{2,0,1:T(8,128)(2,1)} %copy.39) | copy-start | bytes 442372
  112.9 2.5 %copy-start.11 = (bf16[64,16,72]{2,0,1:T(8,128)(2,1)S(1)}, bf16[64,16,72]{2,0,1:T(8,128)(2,1)}, u32[]{:S(2)}) copy-start(bf16[64,16,72]{2,0,1:T(8,128)(2,1)} %copy.47) | copy-start | bytes 442372
  115.4 3.3 %copy-start.6 = (bf16[1,512,1152]{1,2,0:T(8,128)(2,1)S(1)}, bf16[1,512,1152]{1,2,0:T(8,128)(2,1)}, u32[]{:S(2)}) copy-start(bf16[1,512,1152]{1,2,0:T(8,128)(2,1)} %copy.37) | copy-start | bytes 3538948
  115.4 3.3 %copy-start.17 = (f32[16,64,512]{2,1,0:T(8,128)S(1)}, f32[16,64,512]{2,1,0:T(8,128)}, u32[]{:S(2)}) copy-start(f32[16,64,512]{2,1,0:T(8,128)} %get-tuple-element.12) | copy-start | bytes 6291460
  115.4 3.3 %copy-start.19 = (f32[16,72,64]{1,2,0:T(8,128)S(1)}, f32[16,72,64]{1,2,0:T(8,128)}, u32[]{:S(2)}) copy-start(f32[16,72,64]{1,2,0:T(8,128)} %fusion.34) | copy-start | bytes 884740
  118.8 2.5 %copy-start.13 = (f32[64]{0:T(128)S(1)}, f32[64]{0:T(128)}, u32[]{:S(2)}) copy-start(f32[64]{0:T(128)} %broadcast_multiply_fusion.4) | copy-start | bytes 772
  118.8 2.7 %copy-start.8 = (s32[64,1152]{1,0:T(8,128)S(1)}, s32[64,1152]{1,0:T(8,128)}, u32[]{:S(2)}) copy-start(s32[64,1152]{1,0:T(8,128)} %param.14) | copy-start | bytes 884740
  125.3 16.4 %all-to-all-start = ((bf16[16,8,1152]{2,1,0:T(8,128)(2,1)}), bf16[16,8,1152]{2,1,0:T(8,128)(2,1)S(1)}, u32[]{:S(2)}, u32[]{:S(2)}) async-start(bf16[16,8,1152]{2,1,0:T(8,128)(2,1)} %fusion.11), calls=%async_computation | async-start | bytes 589824 | tf_op jit(solution)/shard_map/all_to_all | solution.py:180
  141.7 14.8 %all-to-all-start.2 = ((bf16[16,8,1152]{2,1,0:T(8,128)(2,1)}), bf16[16,8,1152]{2,1,0:T(8,128)(2,1)}, u32[]{:S(2)}, u32[]{:S(2)}) async-start(bf16[16,8,1152]{2,1,0:T(8,128)(2,1)} %fusion.12), calls=%async_computation.2 | async-start | bytes 589824 | tf_op jit(solution)/shard_map/all_to_all | solution.py:181
  170.8 14.1 %all-to-all-start.3 = ((bf16[16,8,1152]{2,1,0:T(8,128)(2,1)}), bf16[16,8,1152]{2,1,0:T(8,128)(2,1)S(1)}, u32[]{:S(2)}, u32[]{:S(2)}) async-start(bf16[16,8,1152]{2,1,0:T(8,128)(2,1)} %fusion.14), calls=%async_computation.3 | async-start | bytes 589824 | tf_op jit(solution)/shard_map/all_to_all | solution.py:83
  185.6 14.7 %all-to-all-start.1 = ((bf16[16,8,1152]{2,1,0:T(8,128)(2,1)}), bf16[16,8,1152]{2,1,0:T(8,128)(2,1)S(1)}, u32[]{:S(2)}, u32[]{:S(2)}) async-start(bf16[16,8,1152]{2,1,0:T(8,128)(2,1)} %fusion.13), calls=%async_computation.1 | async-start | bytes 589824 | tf_op jit(solution)/shard_map/all_to_all | solution.py:82
  (3 other events, 4.2 us)
where the time goes:
time: 203 us; the launch traced here: 202 us
  waiting for transfers between devices  78.5 us (39%)
  matrix products  53.3 us (26%)
  local copies, waits for them, and re-layouts  28.6 us (14%)
  starting transfers between devices  23.1 us (11%)
  other arithmetic  17.5 us (9%)
    ppermute x3, waiting for transfers between devices, from_partner(): return lax.ppermute(block, axis, route)  57.5 us
    dot_general x1, matrix products, owner_partials(): lax.dot_general(act_slope, expert_down, contract, preferred_element_type=...  14.4 us
    dot_general x1, matrix products, owner_partials(): lax.dot_general(act_low, expert_down, contract, preferred_element_type=jn...  8.65 us
    all_to_all x1, waiting for transfers between devices, send_back(): lax.all_to_all(main_part, 'expert', split_axis=0, concat_axis=0, tiled=True)  7.92 us
    all_to_all x1, waiting for transfers between devices, per_device(): lax.all_to_all(outgoing[0], 'expert', split_axis=0, concat_axis=0, tiled=...  7.91 us
    dot_general x1, matrix products, owner_partials(): preact = jnp.dot(main_rows, expert_up, preferred_element_type=jnp.float32)  7.13 us
    concatenate x3, other arithmetic, per_device(): jnp.concatenate([key_set, from_partner(key_set, 'expert', bit_index)], ax...  5.92 us
    all_to_all x1, starting transfers between devices, per_device(): lax.all_to_all(outgoing[0], 'expert', split_axis=0, concat_axis=0, tiled=...  5.85 us
  transfers between devices with their start and end apart: 7, of which 7 were waited for; matrix products, arithmetic and copies ran while one was open for 21% of the time, Pallas kernels for 0%

commit v1 on v0

v1 whole, which is shorter than its diff:
```python
import functools

import jax
import jax.numpy as jnp
from jax import lax
from jax.experimental import pallas as pl
from jax.experimental.pallas import tpu as pltpu
from jax.sharding import PartitionSpec as P

D = 1152
HEADS = 16
EXPERTS = 16
TOP = 2
LENGTH = 512
HEAD_DIM = D // HEADS
PAIR = 16

CUBIC_COEF = 0.044715
TANH_SCALE = 0.7978845608028654
NORM_EPS = 1e-06
LOG2E = 1.4426950408889634
F32 = jnp.float32
BF16 = jnp.bfloat16
MESH = pl.DeviceIdType.MESH


def gelu_pair(preact):
    square = preact * preact
    tanh_value = jnp.tanh(TANH_SCALE * preact * (1.0 + CUBIC_COEF * square))
    half = 0.5 * (1.0 + tanh_value)
    activation = preact * half
    derivative = half + (0.5 * TANH_SCALE) * preact * (1.0 - tanh_value * tanh_value) * (
        1.0 + 3.0 * CUBIC_COEF * square
    )
    return (activation, derivative)


def norm_pair(hidden, tangent):
    average = jnp.mean(hidden, axis=-1, keepdims=True)
    centered = hidden - average
    variance = jnp.mean(centered * centered, axis=-1, keepdims=True)
    inverse = lax.rsqrt(variance + NORM_EPS)
    normed = centered * inverse
    tangent_centered = tangent - jnp.mean(tangent, axis=-1, keepdims=True)
    normed_tangent = inverse * (
        tangent_centered - normed * jnp.mean(normed * tangent_centered, axis=-1, keepdims=True)
    )
    return (normed, normed_tangent)


def slot_choice(ids, gates, lanes, shift):
    tok = ids.shape[0]
    lane = lax.broadcasted_iota(jnp.int32, (tok, lanes), 1)
    named = lane >> shift
    first = ids[:, 0:1] == named
    second = ids[:, 1:2] == named
    has = jnp.where(first, 1.0, jnp.where(second, 1.0, 0.0))
    gate = jnp.where(first, gates[:, 0:1], jnp.where(second, gates[:, 1:2], 0.0))
    row = lax.broadcasted_iota(jnp.int32, (tok, tok), 0)
    column = lax.broadcasted_iota(jnp.int32, (tok, tok), 1)
    earlier = jnp.where(column < row, 1.0, 0.0).astype(BF16)
    rank = jnp.dot(earlier, has.astype(BF16), preferred_element_type=F32)
    picked = jnp.where(rank == (lane & 7).astype(F32), has, 0.0)
    tangent_lane = (lane & 8) != 0
    main = jnp.where(tangent_lane, 0.0, picked)
    slope = jnp.where(tangent_lane, picked, 0.0)
    return main, slope, gate


def kernel(
    n,
    block_ref, bits_ref, q_ref, k_ref, v_ref, dq_ref, dk_ref, dv_ref, ids_ref, gates_ref,
    wo_hbm, up_hbm, down_hbm,
    out_ref, tan_ref, dot_ref,
    wo, up, down,
    pack_send, pack_recv, mix_send, mix_recv, hidden, slots, rows_in, act, made, rows_back,
    load_sem, pack_ss, pack_rs, mix_ss, mix_rs, disp_ss, near_rs, far_rs, back_ss, back_rs,
):
    tok = block_ref.shape[0]
    near = LENGTH // tok
    owners = n // EXPERTS
    hid = up.shape[1]
    cols = D // near
    me = lax.axis_index("expert")
    pos = lax.rem(me, near)
    base = me - pos

    def send(src, dst, send_sem, recv_sem, device):
        pltpu.make_async_remote_copy(
            src_ref=src, dst_ref=dst, send_sem=send_sem, recv_sem=recv_sem,
            device_id={"expert": device}, device_id_type=MESH,
        ).start()

    def wait_bytes(ref, sem):
        pltpu.make_async_copy(ref, ref, sem).wait()

    barrier = pltpu.get_barrier_semaphore()

    @pl.loop(1, n)
    def _(k):
        pl.semaphore_signal(
            barrier, inc=1, device_id={"expert": lax.rem(me + k, n)}, device_id_type=MESH
        )

    loads = [
        pltpu.make_async_copy(wo_hbm, wo, load_sem.at[0]),
        pltpu.make_async_copy(up_hbm, up, load_sem.at[1]),
        pltpu.make_async_copy(down_hbm, down, load_sem.at[2]),
    ]
    for load in loads:
        load.start()

    parts = [ref[...] for ref in (k_ref, dk_ref, dq_ref, q_ref, v_ref, dv_ref)]
    pad = jnp.zeros((tok, pack_send.shape[2] - 6 * cols), BF16)
    for j in range(near):
        pieces = []
        for pair in (parts[0:2], parts[2:4], parts[4:6]):
            for start in range(j * cols, (j + 1) * cols, HEAD_DIM):
                pieces += [part[:, start : start + HEAD_DIM] for part in pair]
        pack_send[j] = jnp.concatenate(pieces + [pad], axis=1)

    pl.semaphore_wait(barrier, n - 1)

    @pl.loop(1, near)
    def _(k):
        j = lax.rem(pos + k, near)
        send(
            pack_send.at[j], pack_recv.at[pl.ds(pl.multiple_of(pos * tok, tok), tok)],
            pack_ss, pack_rs, base + j,
        )

    pack_recv[pl.ds(pl.multiple_of(pos * tok, tok), tok), :] = pack_send[pos]
    wait_bytes(pack_recv.at[pl.ds(0, (near - 1) * tok)], pack_rs)

    local_heads = HEADS // near
    double = 2 * HEAD_DIM
    tail = 4 * cols // 128 * 128
    values_t = pack_recv[:, tail:].T
    tile = 2 * tok

    @pl.loop(0, near // 2)
    def _(i):
        rows = pl.ds(pl.multiple_of(i * tile, tile), tile)
        mains, slopes = [], []
        for h in range(local_heads):
            keys = pack_recv[:, h * double : (h + 1) * double]
            queries = pack_recv[rows, 2 * cols + h * double : 2 * cols + (h + 1) * double]
            alone = jnp.concatenate(
                [queries[:, HEAD_DIM:], jnp.zeros((tile, HEAD_DIM), BF16)], axis=1
            )
            both = lax.dot_general(
                keys, jnp.concatenate([alone, queries], axis=0),
                (((1,), (1,)), ((), ())), preferred_element_type=F32,
            )
            scores, slope = both[:, :tile], both[:, tile:]
            top = jnp.max(scores, axis=0, keepdims=True)
            exponent = jnp.exp2((scores - top) * (HEAD_DIM ** (-0.5) * LOG2E))
            inverse = 1.0 / jnp.sum(exponent, axis=0, keepdims=True)
            weights = exponent * inverse
            middle = jnp.sum(weights * slope, axis=0, keepdims=True)
            weight_slope = weights * ((slope - middle) * HEAD_DIM ** (-0.5))
            joined = jnp.concatenate([weights.astype(BF16), weight_slope.astype(BF16)], axis=1)
            start = 4 * cols - tail + h * double
            mixed = jnp.dot(
                values_t[start : start + double], joined, preferred_element_type=F32
            )
            mains.append(mixed[:HEAD_DIM, :tile])
            slopes.append(mixed[HEAD_DIM:, :tile] + mixed[:HEAD_DIM, tile:])
        main = jnp.concatenate(mains, axis=0)
        slope = jnp.concatenate(slopes, axis=0)
        for half in range(2):
            j = i * 2 + half
            lanes = slice(half * tok, (half + 1) * tok)
            mix_send[j] = jnp.concatenate([main[:, lanes], slope[:, lanes]], axis=1).astype(BF16)

            @pl.when(j != pos)
            def _():
                send(
                    mix_send.at[j], mix_recv.at[pl.ds(pl.multiple_of(pos * cols, 16), cols)],
                    mix_ss, mix_rs, base + j,
                )

    mix_recv[pl.ds(pl.multiple_of(pos * cols, 16), cols), :] = mix_send[pos]
    main_pick, slope_pick, _ = slot_choice(ids_ref[...], gates_ref[...], EXPERTS * PAIR, 4)
    pick = jnp.concatenate([main_pick, slope_pick], axis=0).astype(BF16)
    signs = (2 * bits_ref[...] - 1).astype(F32)
    loads[0].wait()
    wait_bytes(mix_recv.at[pl.ds(0, (near - 1) * cols)], mix_rs)

    hidden[...] = lax.dot_general(
        mix_recv[...], wo[...], (((0,), (0,)), ((), ())), preferred_element_type=F32
    )
    hidden[:tok] += block_ref[...].astype(F32)
    hidden[tok:] += signs
    normed, normed_slope = norm_pair(hidden[:tok], hidden[tok:])
    slots[...] = lax.dot_general(
        pick, jnp.concatenate([normed.astype(BF16), normed_slope.astype(BF16)], axis=0),
        (((0,), (0,)), ((), ())), preferred_element_type=F32,
    ).astype(BF16)

    mine = pl.ds(pl.multiple_of(me * PAIR, PAIR), PAIR)

    def slot_rows(device):
        return pl.ds(pl.multiple_of(device // owners * PAIR, PAIR), PAIR)

    @pl.loop(0, n - near)
    def _(k):
        group = lax.rem(base + near * (1 + k // near), n)
        device = group + lax.rem(pos + k, near)
        send(slots.at[slot_rows(device)], rows_in.at[mine], disp_ss, far_rs, device)

    @pl.loop(1, near)
    def _(k):
        device = base + lax.rem(pos + k, near)
        send(slots.at[slot_rows(device)], rows_in.at[mine], disp_ss, near_rs, device)

    rows_in[mine, :] = slots[slot_rows(me), :]

    up_step = 768 if hid % 768 == 0 else hid
    down_step = 384
    block_rows = near * PAIR

    def expert_block(group):
        start = pl.multiple_of(group * PAIR, block_rows)

        @pl.loop(0, hid // up_step)
        def _(c):
            span = pl.ds(pl.multiple_of(c * up_step, 128), up_step) if hid > up_step else pl.ds(0, hid)
            preact = jnp.dot(
                rows_in[pl.ds(start, block_rows), :], up[:, span], preferred_element_type=F32
            ).reshape(near, PAIR, up_step)
            activation, derivative = gelu_pair(preact[:, :8])
            both = jnp.concatenate([activation, derivative * preact[:, 8:]], axis=1)
            act[:, span] = both.reshape(block_rows, up_step).astype(BF16)

        @pl.loop(0, D // down_step)
        def _(c):
            span = pl.ds(pl.multiple_of(c * down_step, 128), down_step)
            made[pl.ds(start, block_rows), span] = lax.dot_general(
                act[...], down[span, :], (((1,), (1,)), ((), ())), preferred_element_type=F32
            ).astype(BF16)

            @pl.loop(0, near)
            def _(k):
                device = group + lax.rem(pos + k, near)
                source = made.at[pl.ds(pl.multiple_of(device * PAIR, PAIR), PAIR), span]

                @pl.when(device != me)
                def _():
                    send(source, rows_back.at[mine, span], back_ss, back_rs, device)

    loads[1].wait()
    loads[2].wait()
    wait_bytes(rows_in.at[pl.ds(0, (near - 1) * PAIR)], near_rs)
    expert_block(base)
    rows_back[mine, :] = made[mine, :]
    wait_bytes(rows_in.at[pl.ds(0, (n - near) * PAIR)], far_rs)

    @pl.loop(1, n // near)
    def _(g):
        expert_block(lax.rem(base + g * near, n))

    shift = 3 + (PAIR * owners // 8).bit_length() - 1
    main_pick, slope_pick, gate = slot_choice(ids_ref[...], gates_ref[...], n * PAIR, shift)
    mixing = jnp.concatenate([main_pick * gate, slope_pick * gate], axis=0)
    high = mixing.astype(BF16)
    low = (mixing - high.astype(F32)).astype(BF16)
    signs = (2 * bits_ref[...] - 1).astype(F32)
    wait_bytes(rows_back.at[pl.ds(0, (n - 1) * PAIR)], back_rs)

    full = (
        hidden[...]
        + jnp.dot(high, rows_back[...], preferred_element_type=F32)
        + jnp.dot(low, rows_back[...], preferred_element_type=F32)
    )
    out_ref[...] = full[:tok].astype(BF16)
    full_slope = full[tok:]
    tan_ref[...] = full_slope.astype(BF16)
    column = jnp.sum(signs * full_slope, axis=1, keepdims=True) * D ** (-0.5)
    eye = lax.broadcasted_iota(jnp.int32, (tok, tok), 0) == lax.broadcasted_iota(
        jnp.int32, (tok, tok), 1
    )
    dot_ref[...] = jnp.sum(jnp.where(eye, column, 0.0), axis=0, keepdims=True)

    wait_bytes(pack_send.at[pl.ds(0, near - 1)], pack_ss)
    wait_bytes(mix_send.at[pl.ds(0, near - 1)], mix_ss)
    wait_bytes(rows_in.at[pl.ds(0, (n - 1) * PAIR)], disp_ss)
    wait_bytes(made.at[pl.ds(0, (n - 1) * PAIR)], back_ss)


def per_device(
    n,
    block_input,
    probe_bits,
    query_rows,
    key_rows,
    value_rows,
    query_tangent,
    key_tangent,
    value_tangent,
    output_weight,
    expert_up,
    expert_down,
    expert_ids,
    gate_weights,
):
    tok = block_input.shape[0]
    assert tok * TOP // EXPERTS == 8
    hid = expert_up.shape[1]
    near = LENGTH // tok
    cols = D // near
    packed = -(-6 * cols // 128) * 128
    vmem = pl.BlockSpec(memory_space=pltpu.VMEM)
    anywhere = pl.BlockSpec(memory_space=pl.ANY)
    dma = pltpu.SemaphoreType.DMA
    macs = 2 * n * PAIR * D * hid + tok * D * (6 * LENGTH + 2 * D)
    block_output, output_tangent, probe_dot = pl.pallas_call(
        functools.partial(kernel, n),
        out_shape=(
            jax.ShapeDtypeStruct((tok, D), BF16),
            jax.ShapeDtypeStruct((tok, D), BF16),
            jax.ShapeDtypeStruct((1, tok), F32),
        ),
        in_specs=[vmem] * 10 + [anywhere] * 3,
        out_specs=(vmem, vmem, vmem),
        scratch_shapes=[
            pltpu.VMEM((D, D), BF16),
            pltpu.VMEM((D, hid), BF16),
            pltpu.VMEM((D, hid), BF16),
            pltpu.VMEM((near, tok, packed), BF16),
            pltpu.VMEM((LENGTH, packed), BF16),
            pltpu.VMEM((near, cols, 2 * tok), BF16),
            pltpu.VMEM((D, 2 * tok), BF16),
            pltpu.VMEM((2 * tok, D), F32),
            pltpu.VMEM((EXPERTS * PAIR, D), BF16),
            pltpu.VMEM((n * PAIR, D), BF16),
            pltpu.VMEM((near * PAIR, hid), BF16),
            pltpu.VMEM((n * PAIR, D), BF16),
            pltpu.VMEM((n * PAIR, D), BF16),
            dma((3,)),
        ]
        + [dma] * 9,
        compiler_params=pltpu.CompilerParams(
            collective_id=0, has_side_effects=True, vmem_limit_bytes=56 * 1024 * 1024
        ),
        cost_estimate=pl.CostEstimate(
            flops=2 * macs, bytes_accessed=4 * D * hid + 2 * D * D, transcendentals=tok * D * 64
        ),
    )(
        block_input, probe_bits, query_rows, key_rows, value_rows,
        query_tangent, key_tangent, value_tangent, expert_ids, gate_weights,
        output_weight, expert_up, expert_down,
    )
    return (block_output, output_tangent, probe_dot.reshape(tok))


def solution(mesh):
    token_rows = P(("groups", "expert"), None)
    return jax.shard_map(
        functools.partial(per_device, mesh.shape["expert"]),
        mesh=mesh,
        in_specs=(token_rows,) * 8
        + (P(), P(None, "expert"), P(None, "expert"), token_rows, token_rows),
        out_specs=(token_rows, token_rows, P(("groups", "expert"))),
        check_vma=False,
    )
```

time: 203 us -> 71.1 us (0.35)
  waiting for transfers between devices: 78.5 us -> 0 us
  Pallas kernels: 0 us -> 63.1 us
  matrix products: 53.3 us -> 0 us
  starting transfers between devices: 23.1 us -> 0 us
  local copies, waits for them, and re-layouts: 28.6 us -> 7.11 us
  other arithmetic: 17.5 us -> 0 us
    pallas_call x0 -> x1, Pallas kernels: none -> 63.1 us  [per_device(): pl.pallas_call(functools.partial(kernel, n), out_shape=(jax.ShapeDtypeStr...]
    ppermute x3 -> x0, waiting for transfers between devices: 57.5 us -> none  [from_partner(): return lax.ppermute(block, axis, route)]
    dot_general x13 -> x0, matrix products: 50 us -> none  [the longest x1 14.4 us: owner_partials(): lax.dot_general(act_slope, expert_down, contract, preferred_element_type=...]
    all_to_all x4 -> x0, waiting for transfers between devices: 21 us -> none  [the longest x1 7.92 us: send_back(): lax.all_to_all(main_part, 'expert', split_axis=0, concat_axis=0, tiled=True)]
    all_to_all x4 -> x0, starting transfers between devices: 17.8 us -> none  [the longest x1 5.85 us: per_device(): lax.all_to_all(outgoing[0], 'expert', split_axis=0, concat_axis=0, tiled=...]
    slice x5 -> x0, local copies, waits for them, and re-layouts: 12.1 us -> none  [the longest x2 4.75 us: per_device(): key_heads[2]]
    reshape x6 -> x0, local copies, waits for them, and re-layouts: 8.8 us -> none  [the longest x2 3.8 us: per_device(): query_tangent.reshape(row_count, HEADS, head_dim)]
    concatenate x3 -> x0, other arithmetic: 5.92 us -> none  [per_device(): jnp.concatenate([key_set, from_partner(key_set, 'expert', bit_index)], ax...]
  transfers between devices with their start and end apart: 7 -> 0, of which waited for: 7 -> 0; matrix products, arithmetic and copies ran while one was open for 21% -> 0% of each run, Pallas kernels for 0% -> 0%
where the time goes in v1:
time: 71.1 us; the launch traced here: 70.9 us
  Pallas kernels  63.1 us (89%)
  local copies, waits for them, and re-layouts  7.11 us (10%)
    pallas_call x1, Pallas kernels, per_device(): pl.pallas_call(functools.partial(kernel, n), out_shape=(jax.ShapeDtypeStr...  63.1 us
    unnamed x5, local copies, waits for them, and re-layouts  7.11 us

profile of v1, /device:TPU:0, one launch (start us, length us, event | category | flops | bytes accessed | tf_op | source)
XLA Modules:
  0.0 70.9 jit_solution(5564773192693853365)
XLA Ops:
  0.6 1.4 %copy.16.ids_ref = s32[64,2]{1,0:T(8,128)} copy(s32[64,2]{0,1:T(2,128)} %param.24) | data formatting | bytes 1024 | tf_op args[11]
  2.0 1.4 %copy.17.gates_ref = f32[64,2]{1,0:T(8,128)} copy(f32[64,2]{0,1:T(2,128)} %param.25) | data formatting | bytes 1024 | tf_op args[12]
  3.4 63.1 %shard_map.148 = (bf16[64,1152]{1,0:T(8,128)(2,1)}, bf16[64,1152]{1,0:T(8,128)(2,1)}, f32[1,64]{1,0:T(1,128)}) custom-call(bf16[64,1152]{1,0:T(8,128)(2,1)} %block_ref.1, s32[64,1152]{1,0:T(8,128)} %bits_ref.1, bf16[64,1152]{1,0:T(8,128)(2,1)} %q_ref.1, bf16[64,1152]{1,0:T(8,128)(2,1)} %k_ref.1, bf16[64,1152]{1,0:T(8,128)(2,1)} %v_ref.1, ...), custom_call_target="tpu_custom_call" | custom-call | flops 6228541440 | bytes 23887872 | tf_op jit(solution)/shard_map/pallas_call | solution.py:317
  66.5 1.6 %copy.21 = bf16[64,1152]{1,0:T(8,128)(2,1)} copy(bf16[64,1152]{1,0:T(8,128)(2,1)} %get-tuple-element.12) | data formatting | bytes 294912
  68.1 1.6 %copy.22 = bf16[64,1152]{1,0:T(8,128)(2,1)} copy(bf16[64,1152]{1,0:T(8,128)(2,1)} %get-tuple-element.13) | data formatting | bytes 294912
  69.7 1.2 %copy.23 = f32[64]{0:T(128)} copy(f32[64]{0:T(128)} %bitcast.1) | data formatting | bytes 512

commit v2 on v1

v2 whole, which is shorter than its diff:
```python
import functools

import jax
import jax.numpy as jnp
from jax import lax
from jax.experimental import pallas as pl
from jax.experimental.pallas import tpu as pltpu
from jax.sharding import PartitionSpec as P

D = 1152
HEADS = 16
EXPERTS = 16
TOP = 2
LENGTH = 512
HEAD_DIM = D // HEADS
PAIR = 16

CUBIC_COEF = 0.044715
TANH_SCALE = 0.7978845608028654
NORM_EPS = 1e-06
LOG2E = 1.4426950408889634
F32 = jnp.float32
BF16 = jnp.bfloat16
MESH = pl.DeviceIdType.MESH


def gelu_pair(preact):
    square = preact * preact
    tanh_value = jnp.tanh(TANH_SCALE * preact * (1.0 + CUBIC_COEF * square))
    half = 0.5 * (1.0 + tanh_value)
    activation = preact * half
    derivative = half + (0.5 * TANH_SCALE) * preact * (1.0 - tanh_value * tanh_value) * (
        1.0 + 3.0 * CUBIC_COEF * square
    )
    return (activation, derivative)


def norm_pair(hidden, tangent):
    average = jnp.mean(hidden, axis=-1, keepdims=True)
    centered = hidden - average
    variance = jnp.mean(centered * centered, axis=-1, keepdims=True)
    inverse = lax.rsqrt(variance + NORM_EPS)
    normed = centered * inverse
    tangent_centered = tangent - jnp.mean(tangent, axis=-1, keepdims=True)
    normed_tangent = inverse * (
        tangent_centered - normed * jnp.mean(normed * tangent_centered, axis=-1, keepdims=True)
    )
    return (normed, normed_tangent)


def slot_choice(ids, gates, slots, shift):
    tok = ids.shape[1]
    slot = lax.broadcasted_iota(jnp.int32, (slots, tok), 0)
    named = slot >> shift
    first = ids[0:1, :] == named
    second = ids[1:2, :] == named
    has = jnp.where(first, 1.0, jnp.where(second, 1.0, 0.0))
    gate = jnp.where(first, gates[0:1, :], jnp.where(second, gates[1:2, :], 0.0))
    row = lax.broadcasted_iota(jnp.int32, (tok, tok), 0)
    column = lax.broadcasted_iota(jnp.int32, (tok, tok), 1)
    earlier = jnp.where(row < column, 1.0, 0.0).astype(BF16)
    rank = jnp.dot(has.astype(BF16), earlier, preferred_element_type=F32)
    picked = jnp.where(rank == (slot & 7).astype(F32), has, 0.0)
    tangent_slot = (slot & 8) != 0
    main = jnp.where(tangent_slot, 0.0, picked)
    slope = jnp.where(tangent_slot, picked, 0.0)
    return jnp.concatenate([main, slope], axis=1), jnp.concatenate([gate, gate], axis=1)


def kernel(
    n,
    k_hbm, dk_hbm, dq_hbm, q_hbm, v_hbm, dv_hbm, block_hbm, bits_hbm, ids_hbm, gates_hbm,
    wo_hbm, up_hbm, down_hbm,
    out_hbm, tan_hbm, dot_hbm,
    k_ref, dk_ref, dq_ref, q_ref, v_ref, dv_ref, block_ref, bits_ref, ids_ref, gates_ref,
    wo, up, down, out_ref, tan_ref, dot_ref,
    pack_send, pack_recv, probs, mix_send, mix_recv, hidden, pick, mix_high, mix_low,
    slots, rows_in, act, made, rows_back,
    load_sem, out_sem,
    pack_ss, score_rs, value_rs, mix_ss, mix_rs, disp_ss, early_rs, late_rs, back_ss, back_rs,
):
    tok = block_ref.shape[0]
    near = LENGTH // tok
    far = n - near
    owners = n // EXPERTS
    hid = up.shape[1]
    cols = D // near
    me = lax.axis_index("expert")
    pos = lax.rem(me, near)
    base = me - pos

    def send(src, dst, send_sem, recv_sem, device):
        pltpu.make_async_remote_copy(
            src_ref=src, dst_ref=dst, send_sem=send_sem, recv_sem=recv_sem,
            device_id={"expert": device}, device_id_type=MESH,
        ).start()

    def wait_bytes(ref, sem):
        pltpu.make_async_copy(ref, ref, sem).wait()

    barrier = pltpu.get_barrier_semaphore()

    @pl.loop(1, n)
    def _(k):
        pl.semaphore_signal(
            barrier, inc=1, device_id={"expert": lax.rem(me + k, n)}, device_id_type=MESH
        )

    pairs = [
        (k_hbm, k_ref), (dk_hbm, dk_ref), (dq_hbm, dq_ref), (q_hbm, q_ref), (v_hbm, v_ref),
        (dv_hbm, dv_ref), (ids_hbm, ids_ref), (gates_hbm, gates_ref), (block_hbm, block_ref),
        (bits_hbm, bits_ref), (wo_hbm, wo), (up_hbm, up), (down_hbm, down),
    ]
    loads = [
        pltpu.make_async_copy(src, dst, load_sem.at[i]) for i, (src, dst) in enumerate(pairs)
    ]
    for load in loads:
        load.start()
    for load in loads[:6]:
        load.wait()

    parts = [ref[...] for ref in (k_ref, dk_ref, dq_ref, q_ref, v_ref, dv_ref)]
    packed = pack_send.shape[2]
    pad = jnp.zeros((tok, packed - 6 * cols), BF16)
    for j in range(near):
        pieces = []
        for pair in (parts[0:2], parts[2:4], parts[4:6]):
            for start in range(j * cols, (j + 1) * cols, HEAD_DIM):
                pieces += [part[:, start : start + HEAD_DIM] for part in pair]
        pack_send[j] = jnp.concatenate(pieces + [pad], axis=1)

    pl.semaphore_wait(barrier, n - 1)

    score_cols = -(-4 * cols // 128) * 128
    score_part = pl.ds(0, score_cols)
    value_part = pl.ds(score_cols, packed - score_cols)
    my_tokens = pl.ds(pl.multiple_of(pos * tok, tok), tok)
    for part, sem in ((score_part, score_rs), (value_part, value_rs)):

        @pl.loop(1, near)
        def _(k):
            j = lax.rem(pos + k, near)
            send(
                pack_send.at[j, :, part], pack_recv.at[my_tokens, part], pack_ss, sem, base + j
            )

    pack_recv[my_tokens, :] = pack_send[pos]

    loads[6].wait()
    loads[7].wait()
    picked, _ = slot_choice(ids_ref[...], gates_ref[...], EXPERTS * PAIR, 4)
    pick[...] = picked.astype(BF16)
    picked, gate = slot_choice(
        ids_ref[...], gates_ref[...], n * PAIR, 4 + owners.bit_length() - 1
    )
    mixing = (picked * gate).T
    high = mixing.astype(BF16)
    mix_high[...] = high
    mix_low[...] = (mixing - high.astype(F32)).astype(BF16)

    local_heads = HEADS // near
    double = 2 * HEAD_DIM
    tile = 2 * tok
    wait_bytes(pack_recv.at[pl.ds(0, (near - 1) * tok), score_part], score_rs)
    keys = [pack_recv[:, h * double : (h + 1) * double] for h in range(local_heads)]

    @pl.loop(0, near // 2, unroll=2)
    def _(i):
        rows = pl.ds(pl.multiple_of(i * tile, tile), tile)
        for h in range(local_heads):
            queries = pack_recv[rows, 2 * cols + h * double : 2 * cols + (h + 1) * double]
            alone = jnp.concatenate(
                [queries[:, HEAD_DIM:], jnp.zeros((tile, HEAD_DIM), BF16)], axis=1
            )
            both = lax.dot_general(
                keys[h], jnp.concatenate([alone, queries], axis=0),
                (((1,), (1,)), ((), ())), preferred_element_type=F32,
            )
            scores, slope = both[:, :tile], both[:, tile:]
            top = jnp.max(scores, axis=0, keepdims=True)
            exponent = jnp.exp2((scores - top) * (HEAD_DIM ** (-0.5) * LOG2E))
            inverse = 1.0 / jnp.sum(exponent, axis=0, keepdims=True)
            middle = jnp.sum(exponent * slope, axis=0, keepdims=True) * inverse
            probs[i * local_heads + h, :, :tile] = (exponent * inverse).astype(BF16)
            probs[i * local_heads + h, :, tile:] = (
                exponent * (inverse * HEAD_DIM ** (-0.5)) * (slope - middle)
            ).astype(BF16)

    wait_bytes(pack_recv.at[pl.ds(0, (near - 1) * tok), value_part], value_rs)
    tail = 4 * cols // 128 * 128
    values_t = pack_recv[:, tail:].T

    @pl.loop(0, near // 2, unroll=2)
    def _(i):
        mains, slopes = [], []
        for h in range(local_heads):
            start = 4 * cols - tail + h * double
            mixed = jnp.dot(
                values_t[start : start + double], probs[i * local_heads + h],
                preferred_element_type=F32,
            )
            mains.append(mixed[:HEAD_DIM, :tile])
            slopes.append(mixed[HEAD_DIM:, :tile] + mixed[:HEAD_DIM, tile:])
        main = jnp.concatenate(mains, axis=0)
        slope = jnp.concatenate(slopes, axis=0)
        for half in range(2):
            j = i * 2 + half
            lanes = slice(half * tok, (half + 1) * tok)
            mix_send[j] = jnp.concatenate([main[:, lanes], slope[:, lanes]], axis=1).astype(BF16)

            @pl.when(j != pos)
            def _():
                send(
                    mix_send.at[j], mix_recv.at[pl.ds(pl.multiple_of(pos * cols, 16), cols)],
                    mix_ss, mix_rs, base + j,
                )

    mix_recv[pl.ds(pl.multiple_of(pos * cols, 16), cols), :] = mix_send[pos]
    for load in loads[8:11]:
        load.wait()
    wait_bytes(mix_recv.at[pl.ds(0, (near - 1) * cols)], mix_rs)

    hidden[...] = lax.dot_general(
        mix_recv[...], wo[...], (((0,), (0,)), ((), ())), preferred_element_type=F32
    )
    signs = (2 * bits_ref[...] - 1).astype(F32)
    hidden[:tok] += block_ref[...].astype(F32)
    hidden[tok:] += signs
    normed, normed_slope = norm_pair(hidden[:tok], hidden[tok:])
    slots[...] = jnp.dot(
        pick[...],
        jnp.concatenate([normed.astype(BF16), normed_slope.astype(BF16)], axis=0),
        preferred_element_type=F32,
    ).astype(BF16)

    mine = pl.ds(pl.multiple_of(me * PAIR, PAIR), PAIR)

    def slot_rows(device):
        return pl.ds(pl.multiple_of(device // owners * PAIR, PAIR), PAIR)

    def place(t):
        return pl.ds(pl.multiple_of(t * PAIR, PAIR), PAIR)

    def partner(t, sign):
        group = lax.rem(base + n + sign * near * (1 + t // near), n)
        return group + lax.rem(pos + near + sign * lax.rem(t, near), near)

    def dispatch(t, sem):
        device = partner(t, 1)
        send(slots.at[slot_rows(device)], rows_in.at[place(t)], disp_ss, sem, device)

    @pl.loop(0, far // 2)
    def _(t):
        dispatch(t, early_rs)

    @pl.loop(far + 1, n)
    def _(t):
        dispatch(t, late_rs)

    @pl.loop(far // 2, far)
    def _(t):
        dispatch(t, late_rs)

    rows_in[place(far), :] = slots[slot_rows(me), :]

    up_step = 768 if hid % 768 == 0 else hid
    down_step = 384

    def expert_pass(first, last):
        count = (last - first) * PAIR
        block = count if count <= 256 else 4 * PAIR

        @pl.loop(0, count // block)
        def _(b):
            here = pl.ds(pl.multiple_of(b * block, 16), block)
            source = pl.ds(pl.multiple_of(first * PAIR + b * block, 16), block)

            @pl.loop(0, hid // up_step, unroll=min(2, hid // up_step))
            def _(c):
                span = (
                    pl.ds(pl.multiple_of(c * up_step, 128), up_step)
                    if hid > up_step
                    else pl.ds(0, hid)
                )
                preact = jnp.dot(
                    rows_in[source, :], up[:, span], preferred_element_type=F32
                ).reshape(block // PAIR, PAIR, up_step)
                activation, derivative = gelu_pair(preact[:, :8])
                both = jnp.concatenate([activation, derivative * preact[:, 8:]], axis=1)
                act[here, span] = both.reshape(block, up_step).astype(BF16)

        @pl.loop(0, D // down_step)
        def _(c):
            span = pl.ds(pl.multiple_of(c * down_step, 128), down_step)

            @pl.loop(0, count // block)
            def _(b):
                here = pl.ds(pl.multiple_of(b * block, 16), block)
                target = pl.ds(pl.multiple_of(first * PAIR + b * block, 16), block)
                made[target, span] = lax.dot_general(
                    act[here, :], down[span, :], (((1,), (1,)), ((), ())),
                    preferred_element_type=F32,
                ).astype(BF16)

            @pl.loop(first, last)
            def _(t):
                @pl.when(t != far)
                def _():
                    send(
                        made.at[place(t), span], rows_back.at[mine, span],
                        back_ss, back_rs, partner(t, -1),
                    )

    wait_bytes(rows_in.at[pl.ds(0, far // 2 * PAIR)], early_rs)
    loads[11].wait()
    loads[12].wait()
    expert_pass(0, far // 2)
    wait_bytes(rows_in.at[pl.ds(0, (n - 1 - far // 2) * PAIR)], late_rs)
    expert_pass(far // 2, n)
    rows_back[mine, :] = made[place(far), :]
    signs = (2 * bits_ref[...] - 1).astype(F32)
    wait_bytes(rows_back.at[pl.ds(0, (n - 1) * PAIR)], back_rs)

    full = (
        hidden[...]
        + jnp.dot(mix_high[...], rows_back[...], preferred_element_type=F32)
        + jnp.dot(mix_low[...], rows_back[...], preferred_element_type=F32)
    )
    out_ref[...] = full[:tok].astype(BF16)
    full_slope = full[tok:]
    tan_ref[...] = full_slope.astype(BF16)
    column = jnp.sum(signs * full_slope, axis=1, keepdims=True) * D ** (-0.5)
    eye = lax.broadcasted_iota(jnp.int32, (tok, tok), 0) == lax.broadcasted_iota(
        jnp.int32, (tok, tok), 1
    )
    dot_ref[...] = jnp.sum(jnp.where(eye, column, 0.0), axis=0, keepdims=True)
    stores = [
        pltpu.make_async_copy(src, dst, out_sem.at[i])
        for i, (src, dst) in enumerate(
            [(out_ref, out_hbm), (tan_ref, tan_hbm), (dot_ref, dot_hbm)]
        )
    ]
    for store in stores:
        store.start()
    wait_bytes(pack_send.at[pl.ds(0, near - 1)], pack_ss)
    wait_bytes(mix_send.at[pl.ds(0, near - 1)], mix_ss)
    wait_bytes(rows_in.at[pl.ds(0, (n - 1) * PAIR)], disp_ss)
    wait_bytes(made.at[pl.ds(0, (n - 1) * PAIR)], back_ss)
    for store in stores:
        store.wait()


def place_results(a_ref, b_ref, c_ref, x_ref, y_ref, z_ref, sem):
    moves = [
        pltpu.make_async_copy(src, dst, sem.at[i])
        for i, (src, dst) in enumerate([(a_ref, x_ref), (b_ref, y_ref), (c_ref, z_ref)])
    ]
    for move in moves:
        move.start()
    for move in moves:
        move.wait()


def per_device(
    n,
    block_input,
    probe_bits,
    query_rows,
    key_rows,
    value_rows,
    query_tangent,
    key_tangent,
    value_tangent,
    output_weight,
    expert_up,
    expert_down,
    expert_ids,
    gate_weights,
):
    tok = block_input.shape[0]
    assert tok * TOP // EXPERTS == 8
    hid = expert_up.shape[1]
    near = LENGTH // tok
    far = n - near
    cols = D // near
    packed = -(-6 * cols // 128) * 128
    anywhere = pl.BlockSpec(memory_space=pl.ANY)
    dma = pltpu.SemaphoreType.DMA
    macs = 2 * n * PAIR * D * hid + tok * D * (6 * LENGTH + 2 * D)
    results = (
        jax.ShapeDtypeStruct((tok, D), BF16),
        jax.ShapeDtypeStruct((tok, D), BF16),
        jax.ShapeDtypeStruct((1, tok), F32),
    )
    made = pl.pallas_call(
        functools.partial(kernel, n),
        out_shape=results,
        in_specs=[anywhere] * 13,
        out_specs=(anywhere,) * 3,
        scratch_shapes=[pltpu.VMEM((tok, D), BF16)] * 7
        + [
            pltpu.VMEM((tok, D), jnp.int32),
            pltpu.VMEM((TOP, tok), jnp.int32),
            pltpu.VMEM((TOP, tok), F32),
            pltpu.VMEM((D, D), BF16),
            pltpu.VMEM((D, hid), BF16),
            pltpu.VMEM((D, hid), BF16),
            pltpu.VMEM((tok, D), BF16),
            pltpu.VMEM((tok, D), BF16),
            pltpu.VMEM((1, tok), F32),
            pltpu.VMEM((near, tok, packed), BF16),
            pltpu.VMEM((LENGTH, packed), BF16),
            pltpu.VMEM((HEADS // 2, LENGTH, 4 * tok), BF16),
            pltpu.VMEM((near, cols, 2 * tok), BF16),
            pltpu.VMEM((D, 2 * tok), BF16),
            pltpu.VMEM((2 * tok, D), F32),
            pltpu.VMEM((EXPERTS * PAIR, 2 * tok), BF16),
            pltpu.VMEM((2 * tok, n * PAIR), BF16),
            pltpu.VMEM((2 * tok, n * PAIR), BF16),
            pltpu.VMEM((EXPERTS * PAIR, D), BF16),
            pltpu.VMEM((n * PAIR, D), BF16),
            pltpu.VMEM(((n - far // 2) * PAIR, hid), BF16),
            pltpu.VMEM((n * PAIR, D), BF16),
            pltpu.VMEM((n * PAIR, D), BF16),
            dma((13,)),
            dma((3,)),
        ]
        + [dma] * 10,
        compiler_params=pltpu.CompilerParams(
            collective_id=0, has_side_effects=True, vmem_limit_bytes=56 * 1024 * 1024
        ),
        cost_estimate=pl.CostEstimate(
            flops=2 * macs, bytes_accessed=4 * D * hid + 2 * D * D, transcendentals=tok * D * 64
        ),
    )(
        key_rows, key_tangent, query_tangent, query_rows, value_rows, value_tangent,
        block_input, probe_bits, expert_ids.T, gate_weights.T,
        output_weight, expert_up, expert_down,
    )
    block_output, output_tangent, probe_dot = pl.pallas_call(
        place_results,
        out_shape=results,
        in_specs=[anywhere] * 3,
        out_specs=(anywhere,) * 3,
        scratch_shapes=[dma((3,))],
    )(*made)
    return (block_output, output_tangent, probe_dot.reshape(tok))


def solution(mesh):
    token_rows = P(("groups", "expert"), None)
    return jax.shard_map(
        functools.partial(per_device, mesh.shape["expert"]),
        mesh=mesh,
        in_specs=(token_rows,) * 8
        + (P(), P(None, "expert"), P(None, "expert"), token_rows, token_rows),
        out_specs=(token_rows, token_rows, P(("groups", "expert"))),
        check_vma=False,
    )
```

time: 71.1 us -> 67.8 us (0.954)
  local copies, waits for them, and re-layouts: 7.11 us -> 0 us
  Pallas kernels: 63.1 us -> 67 us
    unnamed x5 -> x0, local copies, waits for them, and re-layouts: 7.11 us -> none
    pallas_call x1 -> x2, Pallas kernels: 63.1 us -> 67 us  [the longest x1 57 us: per_device(): pl.pallas_call(functools.partial(kernel, n), out_shape=results, in_specs=...]
where the time goes in v2:
time: 67.8 us; the launch traced here: 67.7 us
  Pallas kernels  67 us (99%)
    pallas_call x1, Pallas kernels, per_device(): pl.pallas_call(functools.partial(kernel, n), out_shape=results, in_specs=...  57 us
    pallas_call x1, Pallas kernels, per_device(): pl.pallas_call(place_results, out_shape=results, in_specs=[anywhere] * 3,...  10.1 us

profile of v2, /device:TPU:0, one launch (start us, length us, event | category | flops | bytes accessed | tf_op | source)
XLA Modules:
  0.0 67.7 jit_solution(11309635439902092612)
XLA Ops:
  0.6 57.0 %shard_map.148 = (bf16[64,1152]{1,0:T(8,128)(2,1)}, bf16[64,1152]{1,0:T(8,128)(2,1)}, f32[1,64]{1,0:T(1,128)}) custom-call(bf16[64,1152]{1,0:T(8,128)(2,1)} %k_hbm.1, bf16[64,1152]{1,0:T(8,128)(2,1)} %dk_hbm.1, bf16[64,1152]{1,0:T(8,128)(2,1)} %dq_hbm.1, bf16[64,1152]{1,0:T(8,128)(2,1)} %q_hbm.1, bf16[64,1152]{1,0:T(8,128)(2,1)} %v_hbm.1, ...), custom_call_target="tpu_custom_call" | custom-call | flops 6228541440 | bytes 23887872 | tf_op jit(solution)/shard_map/pallas_call | solution.py:395
  57.6 10.1 %shard_map.149 = (bf16[64,1152]{1,0:T(8,128)(2,1)}, bf16[64,1152]{1,0:T(8,128)(2,1)}, f32[1,64]{1,0:T(1,128)}) custom-call(bf16[64,1152]{1,0:T(8,128)(2,1)} %get-tuple-element.9.a_ref, bf16[64,1152]{1,0:T(8,128)(2,1)} %get-tuple-element.10.b_ref, f32[1,64]{1,0:T(1,128)} %get-tuple-element.11.c_ref), custom_call_target="tpu_custom_call" | custom-call | tf_op jit(solution)/shard_map/pallas_call | solution.py:440

commit v3 on v2

--- a/solution.py
+++ b/solution.py
@@ -234,39 +234,50 @@
     ).astype(BF16)
 
     mine = pl.ds(pl.multiple_of(me * PAIR, PAIR), PAIR)
+    half = far // 2
 
     def slot_rows(device):
         return pl.ds(pl.multiple_of(device // owners * PAIR, PAIR), PAIR)
 
-    def place(t):
-        return pl.ds(pl.multiple_of(t * PAIR, PAIR), PAIR)
+    def place(u):
+        return pl.ds(pl.multiple_of(u * PAIR, PAIR), PAIR)
 
     def partner(t, sign):
         group = lax.rem(base + n + sign * near * (1 + t // near), n)
         return group + lax.rem(pos + near + sign * lax.rem(t, near), near)
 
-    def dispatch(t, sem):
+    def dispatch(t, u, sem):
         device = partner(t, 1)
-        send(slots.at[slot_rows(device)], rows_in.at[place(t)], disp_ss, sem, device)
-
-    @pl.loop(0, far // 2)
+        send(slots.at[slot_rows(device)], rows_in.at[place(u)], disp_ss, sem, device)
+
+    def give_back(t, u, span):
+        send(
+            made.at[place(u), span], rows_back.at[mine, span],
+            back_ss, back_rs, partner(t, -1),
+        )
+
+    for k in range(near):
+        if k < half:
+            dispatch(k, k, early_rs)
+        else:
+            dispatch(k, k + near, late_rs)
+        if k + 1 < near:
+            dispatch(far + 1 + k, half + 1 + k, early_rs)
+
+    @pl.loop(near, max(near, half))
     def _(t):
-        dispatch(t, early_rs)
-
-    @pl.loop(far + 1, n)
+        dispatch(t, t, early_rs)
+
+    @pl.loop(max(near, half), far)
     def _(t):
-        dispatch(t, late_rs)
-
-    @pl.loop(far // 2, far)
-    def _(t):
-        dispatch(t, late_rs)
-
-    rows_in[place(far), :] = slots[slot_rows(me), :]
+        dispatch(t, t + near, late_rs)
+
+    rows_in[place(half), :] = slots[slot_rows(me), :]
 
     up_step = 768 if hid % 768 == 0 else hid
-    down_step = 384
-
-    def expert_pass(first, last):
+    every = pl.ds(0, D)
+
+    def expert_pass(first, last, send_chunk):
         count = (last - first) * PAIR
         block = count if count <= 256 else 4 * PAIR
 
@@ -289,9 +300,8 @@
                 both = jnp.concatenate([activation, derivative * preact[:, 8:]], axis=1)
                 act[here, span] = both.reshape(block, up_step).astype(BF16)
 
-        @pl.loop(0, D // down_step)
-        def _(c):
-            span = pl.ds(pl.multiple_of(c * down_step, 128), down_step)
+        for start, width in ((0, 512), (512, 512), (1024, 128)):
+            span = pl.ds(start, width)
 
             @pl.loop(0, count // block)
             def _(b):
@@ -302,22 +312,32 @@
                     preferred_element_type=F32,
                 ).astype(BF16)
 
-            @pl.loop(first, last)
-            def _(t):
-                @pl.when(t != far)
-                def _():
-                    send(
-                        made.at[place(t), span], rows_back.at[mine, span],
-                        back_ss, back_rs, partner(t, -1),
-                    )
-
-    wait_bytes(rows_in.at[pl.ds(0, far // 2 * PAIR)], early_rs)
+            send_chunk(span)
+
+    def keep(span):
+        pass
+
+    def send_late(span):
+        @pl.loop(half, far)
+        def _(t):
+            give_back(t, t + near, span)
+
+    wait_bytes(rows_in.at[pl.ds(0, (half + near - 1) * PAIR)], early_rs)
     loads[11].wait()
     loads[12].wait()
-    expert_pass(0, far // 2)
-    wait_bytes(rows_in.at[pl.ds(0, (n - 1 - far // 2) * PAIR)], late_rs)
-    expert_pass(far // 2, n)
-    rows_back[mine, :] = made[place(far), :]
+    expert_pass(0, half + near, keep)
+    wait_bytes(rows_in.at[pl.ds(0, (far - half) * PAIR)], late_rs)
+
+    @pl.loop(0, half)
+    def _(t):
+        give_back(t, t, every)
+
+    @pl.loop(1, near)
+    def _(k):
+        give_back(far + k, half + k, every)
+
+    rows_back[mine, :] = made[place(half), :]
+    expert_pass(half + near, n, send_late)
     signs = (2 * bits_ref[...] - 1).astype(F32)
     wait_bytes(rows_back.at[pl.ds(0, (n - 1) * PAIR)], back_rs)
 
@@ -350,15 +370,24 @@
         store.wait()
 
 
-def place_results(a_ref, b_ref, c_ref, x_ref, y_ref, z_ref, sem):
-    moves = [
-        pltpu.make_async_copy(src, dst, sem.at[i])
-        for i, (src, dst) in enumerate([(a_ref, x_ref), (b_ref, y_ref), (c_ref, z_ref)])
-    ]
-    for move in moves:
-        move.start()
-    for move in moves:
-        move.wait()
+def place_results(a_hbm, b_hbm, c_hbm, x_hbm, y_hbm, z_hbm, a_ref, b_ref, c_ref, sem):
+    moves = []
+    for i, (src, held, dst) in enumerate(
+        [(a_hbm, a_ref, x_hbm), (b_hbm, b_ref, y_hbm), (c_hbm, c_ref, z_hbm)]
+    ):
+        moves.append(
+            (
+                pltpu.make_async_copy(src, held, sem.at[i]),
+                pltpu.make_async_copy(held, dst, sem.at[3 + i]),
+            )
+        )
+    for load, _ in moves:
+        load.start()
+    for load, store in moves:
+        load.wait()
+        store.start()
+    for _, store in moves:
+        store.wait()
 
 
 def per_device(
@@ -419,7 +448,7 @@
             pltpu.VMEM((2 * tok, n * PAIR), BF16),
             pltpu.VMEM((EXPERTS * PAIR, D), BF16),
             pltpu.VMEM((n * PAIR, D), BF16),
-            pltpu.VMEM(((n - far // 2) * PAIR, hid), BF16),
+            pltpu.VMEM(((far // 2 + near) * PAIR, hid), BF16),
             pltpu.VMEM((n * PAIR, D), BF16),
             pltpu.VMEM((n * PAIR, D), BF16),
             dma((13,)),
@@ -442,7 +471,12 @@
         out_shape=results,
         in_specs=[anywhere] * 3,
         out_specs=(anywhere,) * 3,
-        scratch_shapes=[dma((3,))],
+        scratch_shapes=[
+            pltpu.VMEM((tok, D), BF16),
+            pltpu.VMEM((tok, D), BF16),
+            pltpu.VMEM((1, tok), F32),
+            dma((6,)),
+        ],
     )(*made)
     return (block_output, output_tangent, probe_dot.reshape(tok))
 

time: 67.8 us -> 58.8 us (0.87)
  Pallas kernels: 67 us -> 58 us
    pallas_call x1, Pallas kernels: 10.1 us -> 1.7 us  [per_device(): pl.pallas_call(place_results, out_shape=results, in_specs=[anywhere] * 3,...]
    pallas_call x1, Pallas kernels: 57 us -> 56.3 us  [per_device(): pl.pallas_call(functools.partial(kernel, n), out_shape=results, in_specs=...]
where the time goes in v3:
time: 58.8 us; the launch traced here: 58.6 us
  Pallas kernels  58 us (99%)
  between operations  0.64 us (1%)
    pallas_call x1, Pallas kernels, per_device(): pl.pallas_call(functools.partial(kernel, n), out_shape=results, in_specs=...  56.3 us
    pallas_call x1, Pallas kernels, per_device(): pl.pallas_call(place_results, out_shape=results, in_specs=[anywhere] * 3,...  1.7 us

profile of v3, /device:TPU:0, one launch (start us, length us, event | category | flops | bytes accessed | tf_op | source)
XLA Modules:
  0.0 58.6 jit_solution(12050689205188204698)
XLA Ops:
  0.6 56.3 %shard_map.148 = (bf16[64,1152]{1,0:T(8,128)(2,1)}, bf16[64,1152]{1,0:T(8,128)(2,1)}, f32[1,64]{1,0:T(1,128)}) custom-call(bf16[64,1152]{1,0:T(8,128)(2,1)} %k_hbm.1, bf16[64,1152]{1,0:T(8,128)(2,1)} %dk_hbm.1, bf16[64,1152]{1,0:T(8,128)(2,1)} %dq_hbm.1, bf16[64,1152]{1,0:T(8,128)(2,1)} %q_hbm.1, bf16[64,1152]{1,0:T(8,128)(2,1)} %v_hbm.1, ...), custom_call_target="tpu_custom_call" | custom-call | flops 6228541440 | bytes 23887872 | tf_op jit(solution)/shard_map/pallas_call | solution.py:424
  56.9 1.7 %shard_map.149 = (bf16[64,1152]{1,0:T(8,128)(2,1)}, bf16[64,1152]{1,0:T(8,128)(2,1)}, f32[1,64]{1,0:T(1,128)}) custom-call(bf16[64,1152]{1,0:T(8,128)(2,1)} %get-tuple-element.9.a_hbm, bf16[64,1152]{1,0:T(8,128)(2,1)} %get-tuple-element.10.b_hbm, f32[1,64]{1,0:T(1,128)} %get-tuple-element.11.c_hbm), custom_call_target="tpu_custom_call" | custom-call | tf_op jit(solution)/shard_map/pallas_call | solution.py:469

commit v4 on v3

--- a/solution.py
+++ b/solution.py
@@ -100,11 +100,15 @@
 
     barrier = pltpu.get_barrier_semaphore()
 
-    @pl.loop(1, n)
-    def _(k):
-        pl.semaphore_signal(
-            barrier, inc=1, device_id={"expert": lax.rem(me + k, n)}, device_id_type=MESH
-        )
+    def greet(device):
+        pl.semaphore_signal(barrier, inc=1, device_id={"expert": device}, device_id_type=MESH)
+
+    for k in range(1, near):
+        greet(base + lax.rem(pos + k, near))
+
+    @pl.loop(1, n // near)
+    def _(g):
+        greet(lax.rem(me + g * near, n))
 
     pairs = [
         (k_hbm, k_ref), (dk_hbm, dk_ref), (dq_hbm, dq_ref), (q_hbm, q_ref), (v_hbm, v_ref),
@@ -129,7 +133,7 @@
                 pieces += [part[:, start : start + HEAD_DIM] for part in pair]
         pack_send[j] = jnp.concatenate(pieces + [pad], axis=1)
 
-    pl.semaphore_wait(barrier, n - 1)
+    pl.semaphore_wait(barrier, near - 1 + n // near - 1)
 
     score_cols = -(-4 * cols // 128) * 128
     score_part = pl.ds(0, score_cols)
@@ -256,13 +260,12 @@
             back_ss, back_rs, partner(t, -1),
         )
 
-    for k in range(near):
-        if k < half:
-            dispatch(k, k, early_rs)
-        else:
-            dispatch(k, k + near, late_rs)
-        if k + 1 < near:
-            dispatch(far + 1 + k, half + 1 + k, early_rs)
+    for k in range(min(near, half)):
+        dispatch(k, k, early_rs)
+    for k in range(1, near):
+        dispatch(far + k, half + k, early_rs)
+    for k in range(half, near):
+        dispatch(k, k + near, late_rs)
 
     @pl.loop(near, max(near, half))
     def _(t):

time: 58.8 us -> 57.8 us (0.983)
  the two profiles are of different devices: /device:TPU:0 before, /device:TPU:1 now
where the time goes in v4:
time: 57.8 us; the launch traced here: 57.6 us
  Pallas kernels  57 us (99%)
  between operations  0.64 us (1%)
    pallas_call x1, Pallas kernels, per_device(): pl.pallas_call(functools.partial(kernel, n), out_shape=results, in_specs=...  55.3 us
    pallas_call x1, Pallas kernels, per_device(): pl.pallas_call(place_results, out_shape=results, in_specs=[anywhere] * 3,...  1.7 us

profile of v4, /device:TPU:1, one launch (start us, length us, event | category | flops | bytes accessed | tf_op | source)
XLA Modules:
  0.0 57.6 jit_solution(5175681975837698985)
XLA Ops:
  0.6 55.3 %shard_map.148 = (bf16[64,1152]{1,0:T(8,128)(2,1)}, bf16[64,1152]{1,0:T(8,128)(2,1)}, f32[1,64]{1,0:T(1,128)}) custom-call(bf16[64,1152]{1,0:T(8,128)(2,1)} %k_hbm.1, bf16[64,1152]{1,0:T(8,128)(2,1)} %dk_hbm.1, bf16[64,1152]{1,0:T(8,128)(2,1)} %dq_hbm.1, bf16[64,1152]{1,0:T(8,128)(2,1)} %q_hbm.1, bf16[64,1152]{1,0:T(8,128)(2,1)} %v_hbm.1, ...), custom_call_target="tpu_custom_call" | custom-call | flops 6228541440 | bytes 23887872 | tf_op jit(solution)/shard_map/pallas_call | solution.py:427
  55.9 1.7 %shard_map.149 = (bf16[64,1152]{1,0:T(8,128)(2,1)}, bf16[64,1152]{1,0:T(8,128)(2,1)}, f32[1,64]{1,0:T(1,128)}) custom-call(bf16[64,1152]{1,0:T(8,128)(2,1)} %get-tuple-element.9.a_hbm, bf16[64,1152]{1,0:T(8,128)(2,1)} %get-tuple-element.10.b_hbm, f32[1,64]{1,0:T(1,128)} %get-tuple-element.11.c_hbm), custom_call_target="tpu_custom_call" | custom-call | tf_op jit(solution)/shard_map/pallas_call | solution.py:472
